TPU v7x, 32 devices: a whole 2x2x4 slice. The times are simulated.
32 devices in a mesh: seq: 8 (over z, y), head: 4 (over x, core).
Axes of the slice: x: 2, y: 2, z: 4, core: 2. Of those that a mesh axis runs over, the one named last changes fastest.
Arguments:
- queries: bfloat16 [28672, 4096], P('seq', 'head'), may hold values from -6 to 6
- key_rows: bfloat16 [28672, 4096], P('seq', 'head'), may hold values from -6 to 6
- value_rows: bfloat16 [28672, 4096], P('seq', 'head'), may hold values from -6 to 6
- band_reach: int32 [112], P('seq'), may hold values from 1 to 3, as said below
- far_list: int32 [112, 2], P('seq'), may hold values from 0 to 111, as said below
- slopes: float32 [32], P('head'), may hold values from 1e-05 to 0.08
Outputs:
- mixed: bfloat16 [28672, 4096], P(('seq', 'head'))
Inputs may be any that keep to these rules, and one draw needn't show every extreme that they name: Some query block has band_reach exactly 3. `far_list`: block g lies on index g // 14 of seq. Of the 28 far blocks listed for the query blocks of one index of seq, at most 4 lie on any one index, and exactly 4 on some index.
All inputs are finite; a program needn't handle non-finite values.
Results may differ from a plain program's by a relative error of at most 0.0049.
Values may be sent and summed in bfloat16 or wider, within the bound.
A program may use at most 192 MiB of HBM per device.

v0:
```python
import math

import jax
import jax.numpy as jnp
from jax import lax
from jax.sharding import PartitionSpec as P

BT = 256
BAND = 3
FAR = 2


def padded(x, sides, width):
    for axis, dim in sides:
        size, length = (lax.axis_size(axis), x.shape[dim])
        up = [(i, (i + 1) % size) for i in range(size - 1)]
        down = [(j, i) for i, j in up]
        last = lax.slice_in_dim(x, length - width, length, axis=dim)
        first = lax.slice_in_dim(x, 0, width, axis=dim)
        before = lax.ppermute(last, axis, up)
        after = lax.ppermute(first, axis, down)
        x = jnp.concatenate([before, x, after], axis=dim)
    return x


def block_attention(query_rows, key_value, key_pos, key_mask, query_pos, slopes):
    head_count = slopes.shape[0]
    head_size = query_rows.shape[1] // head_count
    queries_h = query_rows.reshape(query_rows.shape[0], head_count, head_size)
    keys_h = key_value[0].reshape(key_value.shape[1], head_count, head_size)
    values_h = key_value[1].reshape(key_value.shape[1], head_count, head_size)
    scores = jnp.einsum("qhd,khd->hqk", queries_h, keys_h, preferred_element_type=jnp.float32) * (
        1.0 / math.sqrt(head_size)
    )
    distance = jnp.abs(query_pos[:, None] - key_pos[None, :]).astype(jnp.float32)
    scores = scores - slopes[:, None, None] * distance[None, :, :]
    scores = jnp.where(key_mask[None, None, :], scores, -jnp.inf)
    row_max = jnp.max(scores, axis=2, keepdims=True)
    raised = jnp.exp(scores - row_max)
    weights = (raised / jnp.sum(raised, axis=2, keepdims=True)).astype(jnp.bfloat16)
    attended = jnp.einsum("hqk,khd->qhd", weights, values_h, preferred_element_type=jnp.float32)
    return attended.astype(jnp.bfloat16).reshape(query_rows.shape[0], head_count * head_size)


def body(queries, key_rows, value_rows, band_reach, far_list, slopes):
    myself = lax.axis_index("seq")
    devices_seq = lax.axis_size("seq")
    tok_rows, channels = key_rows.shape
    blk_dev = tok_rows // BT
    total_blocks = blk_dev * devices_seq
    margin = BAND * BT
    key_value_pair = jnp.stack([key_rows, value_rows])
    requests = far_list.reshape(-1)
    request_count = requests.shape[0]
    capacity = max(2, (request_count + devices_seq - 1) // devices_seq)
    source = requests // blk_dev
    local_blk = requests % blk_dev
    per_source = (source[:, None] == jnp.arange(devices_seq)[None, :]).astype(jnp.int32)
    slot_rank = jnp.sum((jnp.cumsum(per_source, axis=0) - 1) * per_source, axis=1)
    extended = padded(key_value_pair, (("seq", 1),), margin)
    slot_ids = jnp.arange(capacity)
    placed = (per_source[:, :, None] == 1) & (slot_rank[:, None, None] == slot_ids[None, None, :])
    request_table = jnp.sum(jnp.where(placed, local_blk[:, None, None], 0), axis=0)
    asked_for = lax.all_to_all(request_table, "seq", split_axis=0, concat_axis=0, tiled=True)
    local_blocks = key_value_pair.reshape(2, blk_dev, BT, channels)
    outgoing = jnp.take(local_blocks, asked_for, axis=1)
    incoming = lax.all_to_all(outgoing, "seq", split_axis=1, concat_axis=1, tiled=True)
    far_pair = incoming[:, source, slot_rank]
    query_blocks = queries.reshape(blk_dev, BT, channels)
    band_span = 2 * BAND + 1
    offsets = jnp.arange(band_span) - BAND
    within = jnp.arange(BT)

    def attend(local_block):
        block_id = myself * blk_dev + local_block
        band_pair = lax.dynamic_slice_in_dim(extended, local_block * BT, band_span * BT, 1)
        far_part = lax.dynamic_slice_in_dim(far_pair, local_block * FAR, FAR, 1).reshape(
            2, FAR * BT, channels
        )
        key_value = jnp.concatenate([band_pair, far_part], axis=1)
        band_blocks = block_id + offsets
        band_ok = (
            (jnp.abs(offsets) <= band_reach[local_block])
            & (band_blocks >= 0)
            & (band_blocks < total_blocks)
        )
        key_blocks = jnp.concatenate([band_blocks, far_list[local_block]])
        key_ok = jnp.concatenate([band_ok, jnp.ones((FAR,), jnp.bool_)])
        key_pos = (key_blocks[:, None] * BT + within[None, :]).reshape(-1)
        key_mask = jnp.repeat(key_ok, BT)
        return block_attention(
            query_blocks[local_block], key_value, key_pos, key_mask, block_id * BT + within, slopes
        )

    attended = lax.map(attend, jnp.arange(blk_dev))
    mixed_out = attended.reshape(tok_rows, channels)
    return lax.all_to_all(mixed_out, "head", split_axis=0, concat_axis=1, tiled=True)


def solution(mesh):
    in_specs = (
        P("seq", "head"),
        P("seq", "head"),
        P("seq", "head"),
        P("seq"),
        P("seq", None),
        P("head"),
    )
    out_specs = P(("seq", "head"), None)
    return jax.shard_map(body, mesh=mesh, in_specs=in_specs, out_specs=out_specs, check_vma=False)
```

profile of v0, /device:TPU:12, one launch (start us, length us, event | category | flops | bytes accessed | tf_op | source)
XLA Modules:
  0.0 1802.0 jit_solution(11661153123653949652)
XLA Ops:
  9.4 13.2 pad_maximum_fusion.2
  23.0 18.3 %gather_fusion = bf16[32,2,256,1024]{3,2,1,0:T(8,128)(2,1)} fusion(bf16[2,14,256,1024]{3,2,1,0:T(8,128)(2,1)} %pad_maximum_fusion.2, s32[1024]{0:T(1024)S(1)} %pad_clamp_fusion), kind=kCustom, calls=%fused_computation | custom fusion | bytes 67108992 | tf_op jit(solution)/shard_map/jit(_take)/gather | solution.py:66
  41.3 22.8 %fusion.22 = bf16[2,8,4,256,1024]{4,3,2,0,1:T(8,128)(2,1)} fusion(bf16[8,4,2,256,1024]{4,3,2,1,0:T(8,128)(2,1)} %bitcast.62, pred[8,4]{1,0:T(8,128)(4,1)S(1)} %copy.81), kind=kLoop, calls=%fused_computation.38 | loop fusion | flops 16777216 | bytes 67108896 | tf_op jit(solution)/shard_map/jit(_take)/select_n | solution.py:66
  64.1 7.0 all-to-all-start.1
  71.2 10.1 copy.73
  81.2 10.0 copy.74
  102.4 755.2 %collective-permute-done = bf16[2,768,1024]{1,2,0:T(8,128)(2,1)S(1)} collective-permute-done((bf16[2,768,1024]{1,2,0:T(8,128)(2,1)}, bf16[2,768,1024]{1,2,0:T(8,128)(2,1)S(1)}, u32[]{:S(2)}, u32[]{:S(2)}) %collective-permute-start) | collective-permute-done | bytes 3145760 | tf_op jit(solution)/shard_map/ppermute | solution.py:20
  859.4 16.4 pad_maximum_fusion.1
  875.8 23.0 %copy.87 = bf16[2,8,4,256,1024]{4,3,2,1,0:T(8,128)(2,1)} copy(bf16[2,8,4,256,1024]{4,3,2,0,1:T(8,128)(2,1)} %all-to-all-done.1) | data formatting | bytes 67108864 | tf_op jit(solution)/shard_map/all_to_all | solution.py:67
  898.8 21.6 %gather_fusion.1 = bf16[28,2,256,1024]{3,2,1,0:T(8,128)(2,1)} fusion(bf16[2,8,4,256,1024]{4,3,2,1,0:T(8,128)(2,1)} %copy.87, s32[28]{0:T(128)S(1)} %fusion.27), kind=kCustom, calls=%fused_computation.1 | custom fusion | bytes 58720480 | tf_op jit(solution)/shard_map/gather | solution.py:68
  920.4 770.7 %while.14 = (s32[]{:T(128)}, bf16[14,256,1024]{2,1,0:T(8,128)(2,1)}, s32[14]{0:T(128)S(1)}, bf16[2,5120,1024]{1,2,0:T(8,128)(2,1)}, bf16[2,28,256,1024]{3,2,0,1:...) while((s32[]{:T(128)}, ...), condition=%wide.region_6.7_spmd.clone.clone, body=%wide.region_3.6_spmd.clone.clone.sunk | while | flops 2474578944 | bytes 103350344 | solution.py:95
  921.7 6.5 constant_dynamic-slice_fusion.8
  937.8 7.3 pad_maximum_fusion.6
  951.0 12.3 fusion.44
  963.3 11.1 fusion.45
  976.8 6.5 constant_dynamic-slice_fusion.8
  992.8 7.3 pad_maximum_fusion.6
  1006.1 12.3 fusion.44
  1018.4 11.1 fusion.45
  1031.8 6.5 constant_dynamic-slice_fusion.8
  1047.8 7.3 pad_maximum_fusion.6
  1061.1 12.3 fusion.44
  1073.4 11.1 fusion.45
  1086.9 6.5 constant_dynamic-slice_fusion.8
  1102.9 7.3 pad_maximum_fusion.6
  1116.1 12.3 fusion.44
  1128.4 11.1 fusion.45
  1141.9 6.5 constant_dynamic-slice_fusion.8
  1157.9 7.3 pad_maximum_fusion.6
  1171.2 12.3 fusion.44
  1183.5 11.1 fusion.45
  1213.0 7.3 pad_maximum_fusion.6
  1226.2 12.3 fusion.44
  1238.5 11.1 fusion.45
  1268.0 7.3 pad_maximum_fusion.6
  1281.3 12.3 fusion.44
  1293.6 11.1 fusion.45
  1323.0 7.3 pad_maximum_fusion.6
  1336.3 12.3 fusion.44
  1348.6 11.1 fusion.45
  1378.1 7.3 pad_maximum_fusion.6
  1391.3 12.3 fusion.44
  1403.6 11.1 fusion.45
  1433.1 7.3 pad_maximum_fusion.6
  1446.4 12.3 fusion.44
  1458.7 11.1 fusion.45
  1488.2 7.3 pad_maximum_fusion.6
  1501.4 12.3 fusion.44
  1513.7 11.1 fusion.45
  1527.2 6.5 constant_dynamic-slice_fusion.8
  1543.2 7.3 pad_maximum_fusion.6
  1556.5 12.3 fusion.44
  1568.8 11.1 fusion.45
  1582.2 6.7 constant_dynamic-slice_fusion.8
  1598.4 7.3 pad_maximum_fusion.6
  1611.6 12.3 fusion.44
  1624.0 11.1 fusion.45
  1637.4 6.5 constant_dynamic-slice_fusion.8
  1653.4 7.3 pad_maximum_fusion.6
  1666.7 12.3 fusion.44
  1679.0 11.1 fusion.45
  1691.2 89.1 %all_to_all.39 = bf16[4,896,1024]{2,1,0:T(8,128)(2,1)} all-to-all(bf16[4,896,1024]{2,1,0:T(8,128)(2,1)} %bitcast.76), channel_id=1, replica_groups=mesh['seq'=8,'head'=4] {'head'}, dimensions={0} | all-to-all | bytes 14680064 | tf_op jit(solution)/shard_map/all_to_all | solution.py:97
  1780.3 10.9 copy.92
  1791.2 10.8 copy.93
  (329 shorter events, 256.1 us)
Async XLA Ops:
  3.2 19.4 %all-to-all-start = ((s32[8,1,4]{2,1,0:T(1,128)}), s32[8,1,4]{2,1,0:T(1,128)S(1)}, u32[]{:S(2)}, u32[]{:S(2)}) async-start(s32[8,1,4]{2,1,0:T(1,128)} %copy.79), calls=%async_computation | async-start | bytes 8192 | tf_op jit(solution)/shard_map/all_to_all | solution.py:64
  64.1 811.7 %all-to-all-start.1 = ((bf16[2,8,4,256,1024]{4,3,2,0,1:T(8,128)(2,1)}), bf16[2,8,4,256,1024]{4,3,2,0,1:T(8,128)(2,1)}, u32[]{:S(2)}, u32[]{:S(2)}) async-start(bf16[2,8,4,256,1024]{4,3,2,0,1:T(8,128)(2,1)} %fusion.22), calls=%async_computation.1 | async-start | bytes 67108864 | tf_op jit(solution)/shard_map/all_to_all | solution.py:67
  91.2 10.9 copy-start
  96.0 761.6 %collective-permute-start = (bf16[2,768,1024]{1,2,0:T(8,128)(2,1)}, bf16[2,768,1024]{1,2,0:T(8,128)(2,1)S(1)}, u32[]{:S(2)}, u32[]{:S(2)}) collective-permute-start(bf16[2,768,1024]{1,2,0:T(8,128)(2,1)} %get-tuple-element.283), channel_id=1, source_target_pairs={{0,4},{4,8},{8,12},{12,16},{16,20},{20,24},{24,28},{1,5},{5,9},{9,... | collective-permute-start | bytes 9437192 | tf_op jit(solution)/shard_map/ppermute | solution.py:20
  99.2 760.2 %collective-permute-start.1 = (bf16[2,768,1024]{1,2,0:T(8,128)(2,1)}, bf16[2,768,1024]{1,2,0:T(8,128)(2,1)}, u32[]{:S(2)}, u32[]{:S(2)}) collective-permute-start(bf16[2,768,1024]{1,2,0:T(8,128)(2,1)} %get-tuple-element.284), channel_id=1, source_target_pairs={{4,0},{8,4},{12,8},{16,12},{20,16},{24,20},{28,24},{5,1},{9,5},{13... | collective-permute-start | bytes 9437192 | tf_op jit(solution)/shard_map/ppermute | solution.py:21
  898.8 21.6 %copy-start.1 = (s32[14]{0:T(128)S(1)}, s32[14]{0:T(128)}, u32[]{:S(2)}) copy-start(s32[14]{0:T(128)} %param.11) | copy-start | bytes 172
  898.8 21.6 %copy-start.2 = (f32[8]{0:T(128)S(1)}, f32[8]{0:T(128)}, u32[]{:S(2)}) copy-start(f32[8]{0:T(128)} %param.13) | copy-start | bytes 100
where the time goes:
time: 1810 us; the launch traced here: 1800 us
  waiting for transfers between devices  757 us (42%)
  local copies, waits for them, and re-layouts  374 us (21%)
  matrix products  328 us (18%)
  other arithmetic  180 us (10%)
  blocking collectives  89.1 us (5%)
  loops' own time  54.6 us (3%)
  starting transfers between devices  19.3 us (1%)
    ppermute x1, waiting for transfers between devices, padded(): before = lax.ppermute(last, axis, up)  755 us
    sub x14, matrix products, block_attention(): raised = jnp.exp(scores - row_max)  172 us
    dot_general x14, matrix products, block_attention(): jnp.einsum('hqk,khd->qhd', weights, values_h, preferred_element_type=jnp....  156 us
    concatenate x14, other arithmetic, attend(): key_value = jnp.concatenate([band_pair, far_part], axis=1)  102 us
    dynamic_slice x14, local copies, waits for them, and re-layouts, attend(): lax.dynamic_slice_in_dim(extended, local_block * BT, band_span * BT, 1)  91.8 us
    all_to_all x1, blocking collectives, body(): lax.all_to_all(mixed_out, 'head', split_axis=0, concat_axis=1, tiled=True)  89.1 us
    dynamic_slice x28, local copies, waits for them, and re-layouts, attend(): lax.dynamic_slice_in_dim(far_pair, local_block * FAR, FAR, 1)  79.2 us
    another operation x1, loops' own time, body(): attended = lax.map(attend, jnp.arange(blk_dev))  54.6 us
  transfers between devices with their start and end apart: 4, of which 2 were waited for; matrix products, arithmetic and copies ran while one was open for 3% of the time, Pallas kernels for 0%

commit v1 on v0

v1 whole, which is shorter than its diff:
```python
import functools
import math

import jax
import jax.numpy as jnp
from jax import lax
from jax.experimental import pallas as pl
from jax.experimental.pallas import tpu as pltpu
from jax.sharding import PartitionSpec as P

BT = 256
BAND = 3
FAR = 2
DH = 128
LOG2E = math.log2(math.e)
SCALE = LOG2E / math.sqrt(DH)
LOW = -1e30
VMEM = 56 * 2**20


def params():
    return pltpu.CompilerParams(vmem_limit_bytes=VMEM, dimension_semantics=("arbitrary",))


def pack_kernel(asked, k_ref, v_ref, out_ref):
    out_ref[0, 0] = k_ref[...]
    out_ref[0, 1] = v_ref[...]


def pack(asked, keys, values, start, width):
    slots = asked.shape[0]
    at = start // width
    spec = pl.BlockSpec((BT, width), lambda s, asked: (asked[s], at))
    return pl.pallas_call(
        pack_kernel,
        grid_spec=pltpu.PrefetchScalarGridSpec(
            num_scalar_prefetch=1,
            grid=(slots,),
            in_specs=[spec, spec],
            out_specs=pl.BlockSpec((1, 2, BT, width), lambda s, asked: (s, 0, 0, 0)),
        ),
        out_shape=jax.ShapeDtypeStruct((slots, 2, BT, width), keys.dtype),
        compiler_params=params(),
        cost_estimate=pl.CostEstimate(flops=0, bytes_accessed=slots * BT * width * 8, transcendentals=0),
        name="pack",
    )(asked, keys, values)


def distances(gap):
    rows = lax.broadcasted_iota(jnp.int32, (BT, BT), 0)
    cols = lax.broadcasted_iota(jnp.int32, (BT, BT), 1)
    return jnp.abs(rows - cols + gap).astype(jnp.float32)


def visit(heads, slopes, gap, query, key, value, top, total, acc):
    far = distances(gap)
    for h in range(heads):
        lanes = slice(h * DH, (h + 1) * DH)
        s = lax.dot_general(query(lanes), key(lanes), (((1,), (1,)), ((), ())), preferred_element_type=jnp.float32)
        s = s * SCALE - slopes(h) * far
        old = top[h]
        new = jnp.maximum(old, jnp.max(s, axis=1, keepdims=True))
        p = jnp.exp2(s - new)
        shrink = jnp.exp2(old - new)
        top[h] = new
        total[h] = total[h] * shrink + jnp.sum(p, axis=1, keepdims=True)
        acc[:, lanes] = acc[:, lanes] * shrink + jnp.dot(
            p.astype(jnp.bfloat16), value(lanes), preferred_element_type=jnp.float32
        )


def near_kernel(n, heads, reach, slopes, q_ref, k_ref, v_ref, acc, stats, top, total):
    i = pl.program_id(0)
    top[...] = jnp.full_like(top, LOW)
    total[...] = jnp.zeros_like(total)
    acc[...] = jnp.zeros_like(acc)
    wide = reach[i]

    def step(j, carry):
        rows = pl.ds(pl.multiple_of(j * BT, BT), BT)
        visit(
            heads, lambda h: slopes[h], (i - j) * BT,
            lambda c: q_ref[:, c], lambda c: k_ref[rows, c], lambda c: v_ref[rows, c],
            top, total, acc,
        )
        return carry

    lax.fori_loop(jnp.maximum(i - wide, 0), jnp.minimum(i + wide, n - 1) + 1, step, 0)
    lane = lax.broadcasted_iota(jnp.int32, (BT, DH), 1)
    kept = jnp.zeros((BT, DH), jnp.float32)
    for h in range(heads):
        kept = jnp.where(lane == 2 * h, top[h], kept)
        kept = jnp.where(lane == 2 * h + 1, total[h], kept)
    stats[...] = kept


def near(reach, slopes, queries, keys, values):
    rows, channels = keys.shape
    n, heads = rows // BT, channels // DH
    block = pl.BlockSpec((BT, channels), lambda i, *_: (i, 0))
    whole = pl.BlockSpec((rows, channels), lambda i, *_: (0, 0))
    return pl.pallas_call(
        functools.partial(near_kernel, n, heads),
        grid_spec=pltpu.PrefetchScalarGridSpec(
            num_scalar_prefetch=2,
            grid=(n,),
            in_specs=[block, whole, whole],
            out_specs=[block, pl.BlockSpec((BT, DH), lambda i, *_: (i, 0))],
            scratch_shapes=[pltpu.VMEM((heads, BT, 1), jnp.float32)] * 2,
        ),
        out_shape=[
            jax.ShapeDtypeStruct((rows, channels), jnp.float32),
            jax.ShapeDtypeStruct((rows, DH), jnp.float32),
        ],
        compiler_params=params(),
        cost_estimate=pl.CostEstimate(
            flops=rows * 7 * BT * channels * 16, bytes_accessed=rows * channels * 12, transcendentals=rows * 7 * BT * heads
        ),
        name="near",
    )(reach, slopes, queries, keys, values)


def rest_kernel(
    n, heads, first, reach, info, far_list, slot, slopes,
    q_ref, acc_ref, stats_ref, kp, vp, kn, vn, far0, far1, out_ref, top, total, acc,
):
    i = pl.program_id(0)
    me, last = info[0], info[1]
    wide = reach[i]
    acc[...] = acc_ref[...]
    for h in range(heads):
        at = 2 * (first + h)
        top[h] = stats_ref[:, at : at + 1]
        total[h] = stats_ref[:, at + 1 : at + 2]

    def beside(k_ref, v_ref, offset):
        def step(b, carry):
            rows = pl.ds(pl.multiple_of(b * BT, BT), BT)
            visit(
                heads, lambda h: slopes[first + h], (i - offset - b) * BT,
                lambda c: q_ref[:, c], lambda c: k_ref[rows, c], lambda c: v_ref[rows, c],
                top, total, acc,
            )
            return carry

        return step

    lax.fori_loop(jnp.where(me == 0, BAND, jnp.minimum(i + BAND - wide, BAND)), BAND, beside(kp, vp, -BAND), 0)
    lax.fori_loop(0, jnp.where(me == last, 0, jnp.maximum(i + wide + 1 - n, 0)), beside(kn, vn, n), 0)
    for f, ref in enumerate((far0, far1)):
        visit(
            heads, lambda h: slopes[first + h], (me * n + i - far_list[FAR * i + f]) * BT,
            lambda c: q_ref[:, c], lambda c: ref[0, 0, :, c], lambda c: ref[0, 1, :, c],
            top, total, acc,
        )
    for h in range(heads):
        lanes = slice(h * DH, (h + 1) * DH)
        out_ref[:, lanes] = (acc[:, lanes] / total[h]).astype(out_ref.dtype)


def rest(reach, info, far_list, slot, slopes, queries, acc, stats, halos, incoming, start, width):
    rows = queries.shape[0]
    n, heads, at = rows // BT, width // DH, start // width
    block = pl.BlockSpec((BT, width), lambda i, *_: (i, at))
    halo = pl.BlockSpec((BAND * BT, width), lambda i, *_: (0, at))

    def far(f):
        return pl.BlockSpec((1, 2, BT, width), lambda i, reach, info, far_list, slot, slopes: (slot[FAR * i + f], 0, 0, 0))

    return pl.pallas_call(
        functools.partial(rest_kernel, n, heads, start // DH),
        grid_spec=pltpu.PrefetchScalarGridSpec(
            num_scalar_prefetch=5,
            grid=(n,),
            in_specs=[block, block, pl.BlockSpec((BT, DH), lambda i, *_: (i, 0)), halo, halo, halo, halo, far(0), far(1)],
            out_specs=pl.BlockSpec((BT, width), lambda i, *_: (i, 0)),
            scratch_shapes=[pltpu.VMEM((heads, BT, 1), jnp.float32)] * 2 + [pltpu.VMEM((BT, width), jnp.float32)],
        ),
        out_shape=jax.ShapeDtypeStruct((rows, width), queries.dtype),
        compiler_params=params(),
        cost_estimate=pl.CostEstimate(
            flops=rows * 3 * BT * width * 16, bytes_accessed=rows * width * 16, transcendentals=rows * 3 * BT * heads
        ),
        name="rest",
    )(reach, info, far_list, slot, slopes, queries, acc, stats, *halos, incoming, incoming)


def join_kernel(widths, sources, order, *refs):
    out_ref, at, channels = refs[-1], 0, sum(widths)
    for c, width in enumerate(widths):
        for k in range(sources):
            column = pl.multiple_of(order[k] * channels + at, math.gcd(channels, at))
            out_ref[:, pl.ds(column, width)] = refs[c * sources + k][...]
        at += width


def join(order, chunks):
    sources, rows = len(chunks[0]), chunks[0][0].shape[0]
    tile = math.gcd(rows, 128)
    parts = [part for chunk in chunks for part in chunk]
    widths = [chunk[0].shape[1] for chunk in chunks]
    channels = sources * sum(widths)
    return pl.pallas_call(
        functools.partial(join_kernel, widths, sources),
        grid_spec=pltpu.PrefetchScalarGridSpec(
            num_scalar_prefetch=1,
            grid=(rows // tile,),
            in_specs=[pl.BlockSpec((tile, part.shape[1]), lambda r, order: (r, 0)) for part in parts],
            out_specs=pl.BlockSpec((tile, channels), lambda r, order: (r, 0)),
        ),
        out_shape=jax.ShapeDtypeStruct((rows, channels), parts[0].dtype),
        compiler_params=params(),
        name="join",
    )(order, *parts)


def body(queries, key_rows, value_rows, band_reach, far_list, slopes):
    me = lax.axis_index("seq")
    size, head_size = lax.axis_size("seq"), lax.axis_size("head")
    tok_rows, channels = key_rows.shape
    blk_dev, heads = tok_rows // BT, channels // DH
    margin = BAND * BT
    requests = far_list.reshape(-1)
    capacity = max(2, -(-requests.shape[0] // size))
    source = requests // blk_dev
    local_blk = requests % blk_dev
    order = jnp.arange(requests.shape[0])
    earlier = (source[:, None] == source[None, :]) & (order[None, :] < order[:, None])
    rank = jnp.sum(earlier.astype(jnp.int32), axis=1)
    slot = source * capacity + rank
    placed = slot[:, None] == jnp.arange(size * capacity)[None, :]
    table = jnp.sum(jnp.where(placed, local_blk[:, None], 0), axis=0)
    asked = lax.all_to_all(table.reshape(size, capacity), "seq", split_axis=0, concat_axis=0, tiled=True).reshape(-1)
    up = [(i, i + 1) for i in range(size - 1)]
    down = [(j, i) for i, j in up]
    info = jnp.stack([me, jnp.full_like(me, size - 1)]).astype(jnp.int32)
    steep = slopes * LOG2E

    last = heads // 4 if heads % 4 == 0 else heads // 2
    chunks = [(0, channels - last * DH), (channels - last * DH, last * DH)]
    halos = (
        lax.ppermute(key_rows[-margin:], "seq", up),
        lax.ppermute(value_rows[-margin:], "seq", up),
        lax.ppermute(key_rows[:margin], "seq", down),
        lax.ppermute(value_rows[:margin], "seq", down),
    )
    first = pack(asked, key_rows, value_rows, *chunks[0])

    def exchange(packed):
        shape = packed.shape
        packed = packed.reshape(size, capacity, *shape[1:])
        return lax.all_to_all(packed, "seq", split_axis=0, concat_axis=0, tiled=True).reshape(shape)

    arrived = exchange(first)
    second = pack(asked, key_rows, value_rows, *chunks[1])
    acc, stats = near(band_reach, steep, queries, key_rows, value_rows)
    arrived, second, acc, stats, halos = lax.optimization_barrier((arrived, second, acc, stats, halos))
    arrived2 = exchange(second)
    place = lax.axis_index("head")

    def turn(part):
        own = tok_rows // head_size
        got = []
        for k in range(head_size):
            rows = lax.dynamic_slice_in_dim(part, lax.rem(place + k, head_size) * own, own, 0)
            got.append(rows if k == 0 else lax.ppermute(rows, "head", [(i, (i + k) % head_size) for i in range(head_size)]))
        return got

    def finish(far, chunk):
        return turn(rest(band_reach, info, requests, slot, steep, queries, acc, stats, halos, far, *chunk))

    order = lax.rem(place + head_size - jnp.arange(head_size, dtype=jnp.int32), head_size)
    return join(order, [finish(arrived, chunks[0]), finish(arrived2, chunks[1])])


def solution(mesh):
    in_specs = (
        P("seq", "head"),
        P("seq", "head"),
        P("seq", "head"),
        P("seq"),
        P("seq", None),
        P("head"),
    )
    out_specs = P(("seq", "head"), None)
    return jax.shard_map(body, mesh=mesh, in_specs=in_specs, out_specs=out_specs, check_vma=False)
```

time: 1810 us -> 940 us (0.52)
  Pallas kernels: 0 us -> 475 us
  waiting for transfers between devices: 757 us -> 397 us
  local copies, waits for them, and re-layouts: 374 us -> 14.7 us
  matrix products: 328 us -> 0 us
  other arithmetic: 180 us -> 2.62 us
  blocking collectives: 89.1 us -> 10.1 us
  loops' own time: 54.6 us -> 0 us
    pallas_call x0 -> x6, Pallas kernels: none -> 475 us  [the longest x1 253 us: near(): pl.pallas_call(functools.partial(near_kernel, n, heads), grid_spec=pltpu....]
    ppermute x2 -> x10, waiting for transfers between devices: 757 us -> 333 us  [the longest x1 279 us: body(): lax.ppermute(key_rows[-margin:], 'seq', up)]
    dynamic_slice x98 -> x2, local copies, waits for them, and re-layouts: 207 us -> 7.03 us  [turn(): lax.dynamic_slice_in_dim(part, lax.rem(place + k, head_size) * own, own, 0)]
    sub x14 -> x0, matrix products: 172 us -> none  [block_attention(): raised = jnp.exp(scores - row_max)]
    dot_general x14 -> x0, matrix products: 156 us -> none  [block_attention(): jnp.einsum('hqk,khd->qhd', weights, values_h, preferred_element_type=jnp....]
    concatenate x16 -> x0, other arithmetic: 119 us -> none  [the longest x14 102 us: attend(): key_value = jnp.concatenate([band_pair, far_part], axis=1)]
    all_to_all x1, blocking collectives: 89.1 us -> 10.1 us  [body(): lax.all_to_all(table.reshape(size, capacity), 'seq', split_axis=0, concat...]
    all_to_all x2, waiting for transfers between devices: 0.01 us -> 63.5 us  [exchange(): lax.all_to_all(packed, 'seq', split_axis=0, concat_axis=0, tiled=True)]
  transfers between devices with their start and end apart: 4 -> 12, of which waited for: 2 -> 7; matrix products, arithmetic and copies ran while one was open for 3% -> 2% of each run, Pallas kernels for 0% -> 47%
where the time goes in v1:
time: 940 us; the launch traced here: 933 us
  Pallas kernels  475 us (51%)
  waiting for transfers between devices  397 us (42%)
  starting transfers between devices  33.7 us (4%)
  local copies, waits for them, and re-layouts  14.7 us (2%)
  blocking collectives  10.1 us (1%)
    ppermute x1, waiting for transfers between devices, body(): lax.ppermute(key_rows[-margin:], 'seq', up)  279 us
    pallas_call x1, Pallas kernels, near(): pl.pallas_call(functools.partial(near_kernel, n, heads), grid_spec=pltpu....  253 us
    pallas_call x2, Pallas kernels, rest(): pl.pallas_call(functools.partial(rest_kernel, n, heads, start // DH), gri...  163 us
    all_to_all x2, waiting for transfers between devices, exchange(): lax.all_to_all(packed, 'seq', split_axis=0, concat_axis=0, tiled=True)  63.5 us
    pallas_call x2, Pallas kernels, pack(): pl.pallas_call(pack_kernel, grid_spec=pltpu.PrefetchScalarGridSpec(num_sc...  49.6 us
    ppermute x1, waiting for transfers between devices, body(): lax.ppermute(value_rows[-margin:], 'seq', up)  33.7 us
  transfers between devices with their start and end apart: 12, of which 7 were waited for; matrix products, arithmetic and copies ran while one was open for 2% of the time, Pallas kernels for 47%

profile of v1, /device:TPU:12, one launch (start us, length us, event | category | flops | bytes accessed | tf_op | source)
XLA Modules:
  0.0 932.5 jit_solution(11796414064459864768)
XLA Ops:
  0.0 0.8 copy.11
  0.8 0.1 reshape.77.far_list
  0.9 0.0 copy-start.2
  0.9 0.2 convert_reduce_fusion
  1.1 0.0 copy-start.3
  1.1 0.1 select_reduce_fusion
  1.2 0.1 all_to_all.12
  1.3 10.1 %all_to_all.19 = s32[8,1,4]{2,1,0:T(1,128)S(1)} all-to-all(s32[8,1,4]{2,1,0:T(1,128)S(1)} %bitcast.8), channel_id=1, replica_groups=mesh['seq'=8,'head'=4] {'seq'}, dimensions={0} | all-to-all | bytes 256 | tf_op jit(solution)/shard_map/all_to_all | solution.py:233
  11.4 0.5 broadcast.108
  11.9 0.7 reduce.3
  12.6 0.6 reshape.78.asked
  13.2 28.9 %pack.2 = bf16[32,2,256,768]{3,2,1,0:T(8,128)(2,1)} custom-call(s32[32]{0:T(128)} %reshape.78.asked, bf16[3584,1024]{1,0:T(8,128)(2,1)} %k_ref.5, bf16[3584,1024]{1,0:T(8,128)(2,1)} %v_ref.5), custom_call_target="tpu_custom_call" | custom-call | bytes 50331648 | tf_op jit(solution)/shard_map/pack/pallas_call | solution.py:34
  42.1 0.0 copy-done.2
  42.1 0.0 copy-done.3
  42.1 9.9 %all-to-all-start.1 = ((bf16[8,4,2,256,768]{4,3,2,1,0:T(8,128)(2,1)}), bf16[8,4,2,256,768]{4,3,2,1,0:T(8,128)(2,1)}, u32[]{:S(2)}, u32[]{:S(2)}) async-start(bf16[8,4,2,256,768]{4,3,2,1,0:T(8,128)(2,1)} %bitcast.6), calls=%async_computation.1 | async-start | bytes 50331648 | tf_op jit(solution)/shard_map/all_to_all | solution.py:252
  52.0 2.2 fusion.3
  54.2 0.0 copy-start.4
  54.2 3.4 collective-permute-start
  57.6 3.3 fusion.2
  61.0 3.4 collective-permute-start.1
  64.3 2.5 collective-permute-start.2
  66.8 3.4 collective-permute-start.3
  70.2 0.0 copy-done.4
  70.2 0.5 broadcast_multiply_fusion.slopes
  70.7 253.4 %near.1 = (f32[3584,1024]{1,0:T(8,128)}, f32[3584,128]{1,0:T(8,128)}) custom-call(s32[14]{0:T(128)} %reach.5, f32[8]{0:T(128)} %broadcast_multiply_fusion.slopes, bf16[3584,1024]{1,0:T(8,128)(2,1)} %q_ref.5, bf16[3584,1024]{1,0:T(8,128)(2,1)} %k_ref.5, bf16[3584,1024]{1,0:T(8,128)(2,1)} %v_ref.5), custom_call_target="tpu_custom_call" | custom-call | flops 105226698752 | bytes 44040192 | tf_op jit(solution)/shard_map/near/pallas_call | solution.py:102
  324.1 20.6 %pack.3 = bf16[32,2,256,256]{3,2,1,0:T(8,128)(2,1)} custom-call(s32[32]{0:T(128)} %reshape.78.asked, bf16[3584,1024]{1,0:T(8,128)(2,1)} %k_ref.5, bf16[3584,1024]{1,0:T(8,128)(2,1)} %v_ref.5), custom_call_target="tpu_custom_call" | custom-call | bytes 16777216 | tf_op jit(solution)/shard_map/pack/pallas_call | solution.py:34
  344.7 279.2 %collective-permute-done.kp = bf16[768,1024]{1,0:T(8,128)(2,1)S(1)} collective-permute-done((bf16[768,1024]{1,0:T(8,128)(2,1)S(1)}, bf16[768,1024]{1,0:T(8,128)(2,1)S(1)}, u32[]{:S(2)}, u32[]{:S(2)}) %collective-permute-start) | collective-permute-done | bytes 1572896 | tf_op jit(solution)/shard_map/ppermute | solution.py:242
  623.9 0.0 copy-start
  623.9 33.7 %collective-permute-done.1.vp = bf16[768,1024]{1,0:T(8,128)(2,1)S(1)} collective-permute-done((bf16[768,1024]{1,0:T(8,128)(2,1)}, bf16[768,1024]{1,0:T(8,128)(2,1)S(1)}, u32[]{:S(2)}, u32[]{:S(2)}) %collective-permute-start.1) | collective-permute-done | bytes 1572896 | tf_op jit(solution)/shard_map/ppermute | solution.py:243
  657.7 0.0 copy-start.1
  657.7 0.0 collective-permute-done.2.kn
  657.7 1.9 collective-permute-done.3.vn
  659.5 0.0 all-to-all-done.1
  659.6 0.0 copy-done
  659.6 0.0 copy-done.1
  659.6 5.3 all-to-all-start.2
  664.9 0.6 pad_add_fusion.info
  665.5 108.4 %rest.2 = bf16[3584,768]{1,0:T(8,128)(2,1)} custom-call(s32[14]{0:T(128)} %reach.5, s32[2]{0:T(128)} %pad_add_fusion.info, s32[28]{0:T(128)} %copy-done.2, s32[28]{0:T(128)} %copy-done.3, f32[8]{0:T(128)} %broadcast_multiply_fusion.slopes, bf16[3584,1024]{1,0:T(8,128)(2,1)} %q_ref.5, f32[3584,1024]{1,0:T(8,128)} %get-tuple-element.17.acc_ref, ...), custom_call_target="tpu_custom_call" | custom-call | flops 33822867456 | bytes 44040192 | tf_op jit(solution)/shard_map/rest/pallas_call | solution.py:170
  773.9 4.5 constant_dynamic-slice_fusion.4
  778.4 0.0 collective-permute-start.4
  778.4 1.5 collective-permute-start.5
  779.9 1.4 collective-permute-start.6
  781.3 63.5 %all-to-all-done.2 = bf16[8,4,2,256,256]{4,3,2,1,0:T(8,128)(2,1)} async-done(((bf16[8,4,2,256,256]{4,3,2,1,0:T(8,128)(2,1)}), bf16[8,4,2,256,256]{4,3,2,1,0:T(8,128)(2,1)}, u32[]{:S(2)}, u32[]{:S(2)}) %all-to-all-start.2) | async-done | bytes 8388640 | tf_op jit(solution)/shard_map/all_to_all | solution.py:252
  844.8 54.1 %rest.3 = bf16[3584,256]{1,0:T(8,128)(2,1)} custom-call(s32[14]{0:T(128)} %reach.5, s32[2]{0:T(128)} %pad_add_fusion.info, s32[28]{0:T(128)} %copy-done.2, s32[28]{0:T(128)} %copy-done.3, f32[8]{0:T(128)} %broadcast_multiply_fusion.slopes, bf16[3584,1024]{1,0:T(8,128)(2,1)} %q_ref.5, f32[3584,1024]{1,0:T(8,128)} %get-tuple-element.17.acc_ref, ...), custom_call_target="tpu_custom_call" | custom-call | flops 11274289152 | bytes 14680064 | tf_op jit(solution)/shard_map/rest/pallas_call | solution.py:170
  898.9 2.6 constant_dynamic-slice_fusion
  901.5 0.0 collective-permute-start.7
  901.5 1.5 collective-permute-start.8
  903.0 0.0 collective-permute-done.4.refs_1_
  903.0 1.4 collective-permute-start.9
  904.5 0.5 compare_select_fusion.order
  905.0 0.0 collective-permute-done.5.refs_2_
  905.0 0.0 collective-permute-done.6.refs_3_
  905.0 9.1 collective-permute-done.7.refs_5_
  914.1 1.1 collective-permute-done.8.refs_6_
  915.2 8.2 collective-permute-done.9.refs_7_
  923.4 9.2 join.1
  (2 shorter events, 0.0 us)
Async XLA Ops:
  0.9 41.3 %copy-start.2 = (s32[28]{0:T(128)}, s32[28]{0:T(128)S(1)}, u32[]{:S(2)}) copy-start(s32[28]{0:T(128)S(1)} %reshape.77.far_list) | copy-start | bytes 340
  1.1 41.1 %copy-start.3 = (s32[28]{0:T(128)}, s32[28]{0:T(128)S(1)}, u32[]{:S(2)}) copy-start(s32[28]{0:T(128)S(1)} %multiply_add_fusion.slot) | copy-start | bytes 340
  42.1 617.4 %all-to-all-start.1 = ((bf16[8,4,2,256,768]{4,3,2,1,0:T(8,128)(2,1)}), bf16[8,4,2,256,768]{4,3,2,1,0:T(8,128)(2,1)}, u32[]{:S(2)}, u32[]{:S(2)}) async-start(bf16[8,4,2,256,768]{4,3,2,1,0:T(8,128)(2,1)} %bitcast.6), calls=%async_computation.1 | async-start | bytes 50331648 | tf_op jit(solution)/shard_map/all_to_all | solution.py:252
  54.2 16.0 %copy-start.4 = (f32[8]{0:T(128)S(1)}, f32[8]{0:T(128)}, u32[]{:S(2)}) copy-start(f32[8]{0:T(128)} %param.11) | copy-start | bytes 100
  54.2 569.7 %collective-permute-start = (bf16[768,1024]{1,0:T(8,128)(2,1)S(1)}, bf16[768,1024]{1,0:T(8,128)(2,1)S(1)}, u32[]{:S(2)}, u32[]{:S(2)}) collective-permute-start(bf16[768,1024]{1,0:T(8,128)(2,1)S(1)} %get-tuple-element.28), channel_id=1, source_target_pairs={{0,4},{4,8},{8,12},{12,16},{16,20},{20,24},{24,28},{1,5},{5,9},{9,... | collective-permute-start | bytes 4718600 | tf_op jit(solution)/shard_map/ppermute | solution.py:242
  61.0 596.7 %collective-permute-start.1 = (bf16[768,1024]{1,0:T(8,128)(2,1)}, bf16[768,1024]{1,0:T(8,128)(2,1)S(1)}, u32[]{:S(2)}, u32[]{:S(2)}) collective-permute-start(bf16[768,1024]{1,0:T(8,128)(2,1)} %get-tuple-element.26), channel_id=1, source_target_pairs={{0,4},{4,8},{8,12},{12,16},{16,20},{20,24},{24,28},{1,5},{5,9},{9,... | collective-permute-start | bytes 4718600 | tf_op jit(solution)/shard_map/ppermute | solution.py:243
  64.3 593.3 %collective-permute-start.2 = (bf16[768,1024]{1,0:T(8,128)(2,1)S(1)}, bf16[768,1024]{1,0:T(8,128)(2,1)}, u32[]{:S(2)}, u32[]{:S(2)}) collective-permute-start(bf16[768,1024]{1,0:T(8,128)(2,1)S(1)} %get-tuple-element.27), channel_id=1, source_target_pairs={{4,0},{8,4},{12,8},{16,12},{20,16},{24,20},{28,24},{5,1},{9,5},{13... | collective-permute-start | bytes 4718600 | tf_op jit(solution)/shard_map/ppermute | solution.py:244
  66.8 592.7 %collective-permute-start.3 = (bf16[768,1024]{1,0:T(8,128)(2,1)S(1)}, bf16[768,1024]{1,0:T(8,128)(2,1)}, u32[]{:S(2)}, u32[]{:S(2)}) collective-permute-start(bf16[768,1024]{1,0:T(8,128)(2,1)S(1)} %get-tuple-element.25), channel_id=1, source_target_pairs={{4,0},{8,4},{12,8},{16,12},{20,16},{24,20},{28,24},{5,1},{9,5},{13... | collective-permute-start | bytes 4718600 | tf_op jit(solution)/shard_map/ppermute | solution.py:245
  623.9 35.6 %copy-start = (bf16[768,1024]{1,0:T(8,128)(2,1)}, bf16[768,1024]{1,0:T(8,128)(2,1)S(1)}, u32[]{:S(2)}) copy-start(bf16[768,1024]{1,0:T(8,128)(2,1)S(1)} %collective-permute-done.kp) | copy-start | bytes 4718596
  657.7 1.9 copy-start.1
  659.6 185.3 %all-to-all-start.2 = ((bf16[8,4,2,256,256]{4,3,2,1,0:T(8,128)(2,1)}), bf16[8,4,2,256,256]{4,3,2,1,0:T(8,128)(2,1)}, u32[]{:S(2)}, u32[]{:S(2)}) async-start(bf16[8,4,2,256,256]{4,3,2,1,0:T(8,128)(2,1)} %bitcast.7), calls=%async_computation.2 | async-start | bytes 16777216 | tf_op jit(solution)/shard_map/all_to_all | solution.py:252
  778.4 124.7 %collective-permute-start.4 = (bf16[896,768]{1,0:T(8,128)(2,1)}, bf16[896,768]{1,0:T(8,128)(2,1)}, u32[]{:S(2)}, u32[]{:S(2)}) collective-permute-start(bf16[896,768]{1,0:T(8,128)(2,1)} %get-tuple-element.31), channel_id=1, source_target_pairs={{0,1},{1,2},{2,3},{3,0},{4,5},{5,6},{6,7},{7,4},{8,9},{9,10},{10,1... | collective-permute-start | bytes 4128776 | tf_op jit(solution)/shard_map/ppermute | solution.py:266
  778.4 126.6 %collective-permute-start.5 = (bf16[896,768]{1,0:T(8,128)(2,1)S(1)}, bf16[896,768]{1,0:T(8,128)(2,1)}, u32[]{:S(2)}, u32[]{:S(2)}) collective-permute-start(bf16[896,768]{1,0:T(8,128)(2,1)S(1)} %get-tuple-element.30), channel_id=1, source_target_pairs={{0,2},{1,3},{2,0},{3,1},{4,6},{5,7},{6,4},{7,5},{8,10},{9,11},{10,... | collective-permute-start | bytes 4128776 | tf_op jit(solution)/shard_map/ppermute | solution.py:266
  779.9 125.1 %collective-permute-start.6 = (bf16[896,768]{1,0:T(8,128)(2,1)S(1)}, bf16[896,768]{1,0:T(8,128)(2,1)}, u32[]{:S(2)}, u32[]{:S(2)}) collective-permute-start(bf16[896,768]{1,0:T(8,128)(2,1)S(1)} %get-tuple-element.29), channel_id=1, source_target_pairs={{0,3},{1,0},{2,1},{3,2},{4,7},{5,4},{6,5},{7,6},{8,11},{9,8},{10,9... | collective-permute-start | bytes 4128776 | tf_op jit(solution)/shard_map/ppermute | solution.py:266
  901.5 12.6 %collective-permute-start.7 = (bf16[896,256]{1,0:T(8,128)(2,1)}, bf16[896,256]{1,0:T(8,128)(2,1)}, u32[]{:S(2)}, u32[]{:S(2)}) collective-permute-start(bf16[896,256]{1,0:T(8,128)(2,1)} %get-tuple-element.35), channel_id=1, source_target_pairs={{0,1},{1,2},{2,3},{3,0},{4,5},{5,6},{6,7},{7,4},{8,9},{9,10},{10,1... | collective-permute-start | bytes 1376264 | tf_op jit(solution)/shard_map/ppermute | solution.py:266
  901.5 13.7 %collective-permute-start.8 = (bf16[896,256]{1,0:T(8,128)(2,1)}, bf16[896,256]{1,0:T(8,128)(2,1)}, u32[]{:S(2)}, u32[]{:S(2)}) collective-permute-start(bf16[896,256]{1,0:T(8,128)(2,1)} %get-tuple-element.34), channel_id=1, source_target_pairs={{0,2},{1,3},{2,0},{3,1},{4,6},{5,7},{6,4},{7,5},{8,10},{9,11},{10,... | collective-permute-start | bytes 1376264 | tf_op jit(solution)/shard_map/ppermute | solution.py:266
  903.0 20.3 %collective-permute-start.9 = (bf16[896,256]{1,0:T(8,128)(2,1)S(1)}, bf16[896,256]{1,0:T(8,128)(2,1)}, u32[]{:S(2)}, u32[]{:S(2)}) collective-permute-start(bf16[896,256]{1,0:T(8,128)(2,1)S(1)} %get-tuple-element.33), channel_id=1, source_target_pairs={{0,3},{1,0},{2,1},{3,2},{4,7},{5,4},{6,5},{7,6},{8,11},{9,8},{10,9... | collective-permute-start | bytes 1376264 | tf_op jit(solution)/shard_map/ppermute | solution.py:266

commit v2 on v1

--- a/solution.py
+++ b/solution.py
@@ -52,36 +52,38 @@
     return jnp.abs(rows - cols + gap).astype(jnp.float32)
 
 
-def visit(heads, slopes, gap, query, key, value, top, total, acc):
-    far = distances(gap)
+def visit(heads, slopes, query, blocks, top, acc):
+    fars = [distances(gap) for gap, _, _ in blocks]
+    ones = jnp.ones((BT, DH), jnp.bfloat16)
     for h in range(heads):
         lanes = slice(h * DH, (h + 1) * DH)
-        s = lax.dot_general(query(lanes), key(lanes), (((1,), (1,)), ((), ())), preferred_element_type=jnp.float32)
-        s = s * SCALE - slopes(h) * far
+        scores = [
+            lax.dot_general(query(lanes), key(lanes), (((1,), (1,)), ((), ())), preferred_element_type=jnp.float32) * SCALE
+            - slopes(h) * far
+            for far, (_, key, _) in zip(fars, blocks)
+        ]
         old = top[h]
-        new = jnp.maximum(old, jnp.max(s, axis=1, keepdims=True))
-        p = jnp.exp2(s - new)
-        shrink = jnp.exp2(old - new)
+        new = jnp.maximum(old, jnp.max(functools.reduce(jnp.maximum, scores), axis=1, keepdims=True))
         top[h] = new
-        total[h] = total[h] * shrink + jnp.sum(p, axis=1, keepdims=True)
-        acc[:, lanes] = acc[:, lanes] * shrink + jnp.dot(
-            p.astype(jnp.bfloat16), value(lanes), preferred_element_type=jnp.float32
-        )
-
-
-def near_kernel(n, heads, reach, slopes, q_ref, k_ref, v_ref, acc, stats, top, total):
+        summed = acc[h] * jnp.exp2(old - new)
+        for s, (_, _, value) in zip(scores, blocks):
+            p = jnp.exp2(s - new).astype(jnp.bfloat16)
+            both = jnp.concatenate([value(lanes), ones], axis=1)
+            summed = summed + jnp.dot(p, both, preferred_element_type=jnp.float32)
+        acc[h] = summed
+
+
+def near_kernel(n, heads, reach, slopes, q_ref, k_ref, v_ref, acc_ref, stats, top, acc):
     i = pl.program_id(0)
     top[...] = jnp.full_like(top, LOW)
-    total[...] = jnp.zeros_like(total)
     acc[...] = jnp.zeros_like(acc)
     wide = reach[i]
 
     def step(j, carry):
         rows = pl.ds(pl.multiple_of(j * BT, BT), BT)
         visit(
-            heads, lambda h: slopes[h], (i - j) * BT,
-            lambda c: q_ref[:, c], lambda c: k_ref[rows, c], lambda c: v_ref[rows, c],
-            top, total, acc,
+            heads, lambda h: slopes[h], lambda c: q_ref[:, c],
+            [((i - j) * BT, lambda c: k_ref[rows, c], lambda c: v_ref[rows, c])], top, acc,
         )
         return carry
 
@@ -90,7 +92,8 @@
     kept = jnp.zeros((BT, DH), jnp.float32)
     for h in range(heads):
         kept = jnp.where(lane == 2 * h, top[h], kept)
-        kept = jnp.where(lane == 2 * h + 1, total[h], kept)
+        kept = jnp.where(lane == 2 * h + 1, acc[h, :, DH:], kept)
+        acc_ref[:, h * DH : (h + 1) * DH] = acc[h, :, :DH]
     stats[...] = kept
 
 
@@ -106,7 +109,7 @@
             grid=(n,),
             in_specs=[block, whole, whole],
             out_specs=[block, pl.BlockSpec((BT, DH), lambda i, *_: (i, 0))],
-            scratch_shapes=[pltpu.VMEM((heads, BT, 1), jnp.float32)] * 2,
+            scratch_shapes=[pltpu.VMEM((heads, BT, 1), jnp.float32), pltpu.VMEM((heads, BT, 2 * DH), jnp.float32)],
         ),
         out_shape=[
             jax.ShapeDtypeStruct((rows, channels), jnp.float32),
@@ -122,24 +125,23 @@
 
 def rest_kernel(
     n, heads, first, reach, info, far_list, slot, slopes,
-    q_ref, acc_ref, stats_ref, kp, vp, kn, vn, far0, far1, out_ref, top, total, acc,
+    q_ref, acc_ref, stats_ref, kp, vp, kn, vn, far0, far1, out_ref, top, acc,
 ):
     i = pl.program_id(0)
     me, last = info[0], info[1]
     wide = reach[i]
-    acc[...] = acc_ref[...]
     for h in range(heads):
         at = 2 * (first + h)
         top[h] = stats_ref[:, at : at + 1]
-        total[h] = stats_ref[:, at + 1 : at + 2]
+        acc[h, :, :DH] = acc_ref[:, h * DH : (h + 1) * DH]
+        acc[h, :, DH:] = jnp.broadcast_to(stats_ref[:, at + 1 : at + 2], (BT, DH))
 
     def beside(k_ref, v_ref, offset):
         def step(b, carry):
             rows = pl.ds(pl.multiple_of(b * BT, BT), BT)
             visit(
-                heads, lambda h: slopes[first + h], (i - offset - b) * BT,
-                lambda c: q_ref[:, c], lambda c: k_ref[rows, c], lambda c: v_ref[rows, c],
-                top, total, acc,
+                heads, lambda h: slopes[first + h], lambda c: q_ref[:, c],
+                [((i - offset - b) * BT, lambda c: k_ref[rows, c], lambda c: v_ref[rows, c])], top, acc,
             )
             return carry
 
@@ -147,15 +149,13 @@
 
     lax.fori_loop(jnp.where(me == 0, BAND, jnp.minimum(i + BAND - wide, BAND)), BAND, beside(kp, vp, -BAND), 0)
     lax.fori_loop(0, jnp.where(me == last, 0, jnp.maximum(i + wide + 1 - n, 0)), beside(kn, vn, n), 0)
-    for f, ref in enumerate((far0, far1)):
-        visit(
-            heads, lambda h: slopes[first + h], (me * n + i - far_list[FAR * i + f]) * BT,
-            lambda c: q_ref[:, c], lambda c: ref[0, 0, :, c], lambda c: ref[0, 1, :, c],
-            top, total, acc,
-        )
-    for h in range(heads):
-        lanes = slice(h * DH, (h + 1) * DH)
-        out_ref[:, lanes] = (acc[:, lanes] / total[h]).astype(out_ref.dtype)
+    listed = [
+        ((me * n + i - far_list[FAR * i + f]) * BT, lambda c, ref=ref: ref[0, 0, :, c], lambda c, ref=ref: ref[0, 1, :, c])
+        for f, ref in enumerate((far0, far1))
+    ]
+    visit(heads, lambda h: slopes[first + h], lambda c: q_ref[:, c], listed, top, acc)
+    for h in range(heads):
+        out_ref[:, h * DH : (h + 1) * DH] = (acc[h, :, :DH] / acc[h, :, DH:]).astype(out_ref.dtype)
 
 
 def rest(reach, info, far_list, slot, slopes, queries, acc, stats, halos, incoming, start, width):
@@ -174,7 +174,7 @@
             grid=(n,),
             in_specs=[block, block, pl.BlockSpec((BT, DH), lambda i, *_: (i, 0)), halo, halo, halo, halo, far(0), far(1)],
             out_specs=pl.BlockSpec((BT, width), lambda i, *_: (i, 0)),
-            scratch_shapes=[pltpu.VMEM((heads, BT, 1), jnp.float32)] * 2 + [pltpu.VMEM((BT, width), jnp.float32)],
+            scratch_shapes=[pltpu.VMEM((heads, BT, 1), jnp.float32), pltpu.VMEM((heads, BT, 2 * DH), jnp.float32)],
         ),
         out_shape=jax.ShapeDtypeStruct((rows, width), queries.dtype),
         compiler_params=params(),
@@ -236,26 +236,40 @@
     info = jnp.stack([me, jnp.full_like(me, size - 1)]).astype(jnp.int32)
     steep = slopes * LOG2E
 
-    last = heads // 4 if heads % 4 == 0 else heads // 2
-    chunks = [(0, channels - last * DH), (channels - last * DH, last * DH)]
+    most = max(heads - 2, 1)
+    chunks = [(0, most * DH)] + [(h * DH, DH) for h in range(most, heads)]
     halos = (
         lax.ppermute(key_rows[-margin:], "seq", up),
         lax.ppermute(value_rows[-margin:], "seq", up),
         lax.ppermute(key_rows[:margin], "seq", down),
         lax.ppermute(value_rows[:margin], "seq", down),
     )
-    first = pack(asked, key_rows, value_rows, *chunks[0])
+    packed = [pack(asked, key_rows, value_rows, *chunk) for chunk in chunks]
+    packed[0], *keys_beside = lax.optimization_barrier((packed[0], halos[0], halos[2]))
 
     def exchange(packed):
         shape = packed.shape
-        packed = packed.reshape(size, capacity, *shape[1:])
-        return lax.all_to_all(packed, "seq", split_axis=0, concat_axis=0, tiled=True).reshape(shape)
-
-    arrived = exchange(first)
-    second = pack(asked, key_rows, value_rows, *chunks[1])
+        blocks = packed.reshape(size, capacity, *shape[1:])
+        return lax.all_to_all(blocks, "seq", split_axis=0, concat_axis=0, tiled=True).reshape(shape)
+
     acc, stats = near(band_reach, steep, queries, key_rows, value_rows)
-    arrived, second, acc, stats, halos = lax.optimization_barrier((arrived, second, acc, stats, halos))
-    arrived2 = exchange(second)
+    arrived = [exchange(packed[0])]
+    halos = (keys_beside[0], halos[1], keys_beside[1], halos[3])
+
+    def finish(later):
+        return rest(
+            band_reach, info, requests, slot, steep, queries, acc, stats, halos, arrived[later], *chunks[later]
+        )
+
+    done = []
+    for later in range(1, len(chunks)):
+        if later > 1:
+            done.append(finish(later - 2))
+        arrived[-1], packed[later], acc, stats, halos, done = lax.optimization_barrier(
+            (arrived[-1], packed[later], acc, stats, halos, done)
+        )
+        arrived.append(exchange(packed[later]))
+    done += [finish(later) for later in range(len(done), len(chunks))]
     place = lax.axis_index("head")
 
     def turn(part):
@@ -266,11 +280,8 @@
             got.append(rows if k == 0 else lax.ppermute(rows, "head", [(i, (i + k) % head_size) for i in range(head_size)]))
         return got
 
-    def finish(far, chunk):
-        return turn(rest(band_reach, info, requests, slot, steep, queries, acc, stats, halos, far, *chunk))
-
     order = lax.rem(place + head_size - jnp.arange(head_size, dtype=jnp.int32), head_size)
-    return join(order, [finish(arrived, chunks[0]), finish(arrived2, chunks[1])])
+    return join(order, [turn(part) for part in done])
 
 
 def solution(mesh):

time: 940 us -> 940 us (level)
  Pallas kernels: 475 us -> 346 us
  waiting for transfers between devices: 397 us -> 459 us
  blocking collectives: 10.1 us -> 65.6 us
    ppermute x1, waiting for transfers between devices: 33.7 us -> 371 us  [body(): lax.ppermute(value_rows[-margin:], 'seq', up)]
    ppermute x1, waiting for transfers between devices: 279 us -> 0.01 us  [body(): lax.ppermute(key_rows[-margin:], 'seq', up)]
    pallas_call x1, Pallas kernels: 253 us -> 174 us  [near(): pl.pallas_call(functools.partial(near_kernel, n, heads), grid_spec=pltpu....]
    pallas_call x2 -> x3, Pallas kernels: 163 us -> 96.8 us  [rest(): pl.pallas_call(functools.partial(rest_kernel, n, heads, start // DH), gri...]
    all_to_all x1, blocking collectives: 10.1 us -> 65.6 us  [body(): lax.all_to_all(table.reshape(size, capacity), 'seq', split_axis=0, concat...]
    all_to_all x2 -> x3, waiting for transfers between devices: 63.5 us -> 32.8 us  [exchange(): lax.all_to_all(blocks, 'seq', split_axis=0, concat_axis=0, tiled=True)]
    ppermute x6 -> x9, waiting for transfers between devices: 18.4 us -> 49.1 us  [turn(): lax.ppermute(rows, 'head', [(i, (i + k) % head_size) for i in range(head_...]
    pallas_call x2 -> x3, Pallas kernels: 49.6 us -> 65.7 us  [pack(): pl.pallas_call(pack_kernel, grid_spec=pltpu.PrefetchScalarGridSpec(num_sc...]
  transfers between devices with their start and end apart: 12 -> 16, of which waited for: 7 -> 8; matrix products, arithmetic and copies ran while one was open for 2% -> 2% of each run, Pallas kernels for 47% -> 36%
where the time goes in v2:
time: 940 us; the launch traced here: 930 us
  waiting for transfers between devices  459 us (49%)
  Pallas kernels  346 us (37%)
  blocking collectives  65.6 us (7%)
  starting transfers between devices  37.7 us (4%)
  local copies, waits for them, and re-layouts  19.2 us (2%)
    ppermute x1, waiting for transfers between devices, body(): lax.ppermute(value_rows[-margin:], 'seq', up)  371 us
    pallas_call x1, Pallas kernels, near(): pl.pallas_call(functools.partial(near_kernel, n, heads), grid_spec=pltpu....  174 us
    pallas_call x3, Pallas kernels, rest(): pl.pallas_call(functools.partial(rest_kernel, n, heads, start // DH), gri...  96.8 us
    pallas_call x3, Pallas kernels, pack(): pl.pallas_call(pack_kernel, grid_spec=pltpu.PrefetchScalarGridSpec(num_sc...  65.7 us
    all_to_all x1, blocking collectives, body(): lax.all_to_all(table.reshape(size, capacity), 'seq', split_axis=0, concat...  65.6 us
    ppermute x9, waiting for transfers between devices, turn(): lax.ppermute(rows, 'head', [(i, (i + k) % head_size) for i in range(head_...  49.1 us
    all_to_all x3, waiting for transfers between devices, exchange(): lax.all_to_all(blocks, 'seq', split_axis=0, concat_axis=0, tiled=True)  32.8 us
  transfers between devices with their start and end apart: 16, of which 8 were waited for; matrix products, arithmetic and copies ran while one was open for 2% of the time, Pallas kernels for 36%

profile of v2, /device:TPU:12, one launch (start us, length us, event | category | flops | bytes accessed | tf_op | source)
XLA Modules:
  0.0 930.1 jit_solution(11136840706995545519)
XLA Ops:
  0.0 3.9 fusion.3
  3.9 3.4 collective-permute-start
  7.3 2.4 collective-permute-start.1
  9.8 0.0 copy-done.10
  9.8 0.1 copy.11
  9.9 0.1 reshape.83.far_list
  9.9 0.0 copy-start.8
  10.0 0.2 convert_reduce_fusion
  10.2 0.1 select_reduce_fusion
  10.3 0.1 all_to_all.15
  10.3 65.6 %all_to_all.24 = s32[8,1,4]{2,1,0:T(1,128)S(1)} all-to-all(s32[8,1,4]{2,1,0:T(1,128)S(1)} %bitcast.11), channel_id=1, replica_groups=mesh['seq'=8,'head'=4] {'seq'}, dimensions={0} | all-to-all | bytes 256 | tf_op jit(solution)/shard_map/all_to_all | solution.py:233
  75.9 0.6 broadcast.108
  76.5 0.7 reduce.3
  77.2 0.6 reshape.84.asked
  77.9 29.4 %pack.3 = bf16[32,2,256,768]{3,2,1,0:T(8,128)(2,1)} custom-call(s32[32]{0:T(128)} %reshape.84.asked, bf16[3584,1024]{1,0:T(8,128)(2,1)} %k_ref.7, bf16[3584,1024]{1,0:T(8,128)(2,1)} %v_ref.7), custom_call_target="tpu_custom_call" | custom-call | bytes 50331648 | tf_op jit(solution)/shard_map/pack/pallas_call | solution.py:34
  107.3 0.0 collective-permute-done.kp
  107.3 0.0 collective-permute-done.1.kn
  107.3 1.1 copy-done
  108.4 0.5 copy-done.1
  108.9 6.4 all-to-all-start.1
  115.3 0.0 copy-start.11
  115.3 2.2 fusion.2
  117.5 4.7 collective-permute-start.2
  122.2 1.9 collective-permute-start.3
  124.1 0.6 broadcast_multiply_fusion.slopes
  124.7 174.0 %near.1 = (f32[3584,1024]{1,0:T(8,128)}, f32[3584,128]{1,0:T(8,128)}) custom-call(s32[14]{0:T(128)} %reach.7, f32[8]{0:T(128)} %broadcast_multiply_fusion.slopes, bf16[3584,1024]{1,0:T(8,128)(2,1)} %q_ref.7, bf16[3584,1024]{1,0:T(8,128)(2,1)} %k_ref.7, bf16[3584,1024]{1,0:T(8,128)(2,1)} %v_ref.7), custom_call_target="tpu_custom_call" | custom-call | flops 105226698752 | bytes 44040192 | tf_op jit(solution)/shard_map/near/pallas_call | solution.py:105
  298.7 18.1 %pack.4 = bf16[32,2,256,128]{3,2,1,0:T(8,128)(2,1)} custom-call(s32[32]{0:T(128)} %reshape.84.asked, bf16[3584,1024]{1,0:T(8,128)(2,1)} %k_ref.7, bf16[3584,1024]{1,0:T(8,128)(2,1)} %v_ref.7), custom_call_target="tpu_custom_call" | custom-call | bytes 8388608 | tf_op jit(solution)/shard_map/pack/pallas_call | solution.py:34
  316.9 371.2 %collective-permute-done.2.vp = bf16[768,1024]{1,0:T(8,128)(2,1)S(1)} collective-permute-done((bf16[768,1024]{1,0:T(8,128)(2,1)S(1)}, bf16[768,1024]{1,0:T(8,128)(2,1)S(1)}, u32[]{:S(2)}, u32[]{:S(2)}) %collective-permute-start.2) | collective-permute-done | bytes 1572896 | tf_op jit(solution)/shard_map/ppermute | solution.py:243
  688.0 5.8 collective-permute-done.3.vn
  693.9 0.0 all-to-all-done.1
  693.9 1.2 copy-done.3
  695.0 4.5 all-to-all-start.2
  699.6 0.7 pad_add_fusion.info
  700.2 18.1 %pack.5 = bf16[32,2,256,128]{3,2,1,0:T(8,128)(2,1)} custom-call(s32[32]{0:T(128)} %reshape.84.asked, bf16[3584,1024]{1,0:T(8,128)(2,1)} %k_ref.7, bf16[3584,1024]{1,0:T(8,128)(2,1)} %v_ref.7), custom_call_target="tpu_custom_call" | custom-call | bytes 8388608 | tf_op jit(solution)/shard_map/pack/pallas_call | solution.py:34
  718.4 55.6 %rest.3 = bf16[3584,768]{1,0:T(8,128)(2,1)} custom-call(s32[14]{0:T(128)} %reach.7, s32[2]{0:T(128)} %pad_add_fusion.info, s32[28]{0:T(128)} %copy-done.8, s32[28]{0:T(128)} %copy-done.9, f32[8]{0:T(128)} %broadcast_multiply_fusion.slopes, bf16[3584,1024]{1,0:T(8,128)(2,1)} %q_ref.7, f32[3584,1024]{1,0:T(8,128)} %get-tuple-element.41.acc_ref, ...), custom_call_target="tpu_custom_call" | custom-call | flops 33822867456 | bytes 44040192 | tf_op jit(solution)/shard_map/rest/pallas_call | solution.py:170
  773.9 14.8 %all-to-all-done.2 = bf16[8,4,2,256,128]{4,3,2,1,0:T(8,128)(2,1)} async-done(((bf16[8,4,2,256,128]{4,3,2,1,0:T(8,128)(2,1)}), bf16[8,4,2,256,128]{4,3,2,1,0:T(8,128)(2,1)}, u32[]{:S(2)}, u32[]{:S(2)}) %all-to-all-start.2) | async-done | bytes 4194336 | tf_op jit(solution)/shard_map/all_to_all | solution.py:253
  788.7 7.8 all-to-all-start.3
  796.5 4.5 constant_dynamic-slice_fusion.8
  801.0 0.0 collective-permute-start.4
  801.0 1.5 collective-permute-start.5
  802.5 1.4 collective-permute-start.6
  804.0 20.6 %rest.4 = bf16[3584,128]{1,0:T(8,128)(2,1)} custom-call(s32[14]{0:T(128)} %reach.7, s32[2]{0:T(128)} %pad_add_fusion.info, s32[28]{0:T(128)} %copy-done.8, s32[28]{0:T(128)} %copy-done.9, f32[8]{0:T(128)} %broadcast_multiply_fusion.slopes, bf16[3584,1024]{1,0:T(8,128)(2,1)} %q_ref.7, f32[3584,1024]{1,0:T(8,128)} %get-tuple-element.41.acc_ref, ...), custom_call_target="tpu_custom_call" | custom-call | flops 5637144576 | bytes 7340032 | tf_op jit(solution)/shard_map/rest/pallas_call | solution.py:170
  824.6 2.2 constant_dynamic-slice_fusion.4
  826.7 0.0 collective-permute-start.7
  826.8 0.6 collective-permute-start.8
  827.3 40.5 %collective-permute-done.7.refs_5_ = bf16[896,128]{1,0:T(8,128)(2,1)S(1)} collective-permute-done((bf16[896,128]{1,0:T(8,128)(2,1)S(1)}, bf16[896,128]{1,0:T(8,128)(2,1)S(1)}, u32[]{:S(2)}, u32[]{:S(2)}) %collective-permute-start.7) | collective-permute-done | bytes 229408 | tf_op jit(solution)/shard_map/ppermute | solution.py:280
  867.8 0.0 collective-permute-start.9
  867.8 18.0 %all-to-all-done.3 = bf16[8,4,2,256,128]{4,3,2,1,0:T(8,128)(2,1)} async-done(((bf16[8,4,2,256,128]{4,3,2,1,0:T(8,128)(2,1)}), bf16[8,4,2,256,128]{4,3,2,1,0:T(8,128)(2,1)}, u32[]{:S(2)}, u32[]{:S(2)}) %all-to-all-start.3) | async-done | bytes 4194336 | tf_op jit(solution)/shard_map/all_to_all | solution.py:253
  885.8 20.6 %rest.5 = bf16[3584,128]{1,0:T(8,128)(2,1)} custom-call(s32[14]{0:T(128)} %reach.7, s32[2]{0:T(128)} %pad_add_fusion.info, s32[28]{0:T(128)} %copy-done.8, s32[28]{0:T(128)} %copy-done.9, f32[8]{0:T(128)} %broadcast_multiply_fusion.slopes, bf16[3584,1024]{1,0:T(8,128)(2,1)} %q_ref.7, f32[3584,1024]{1,0:T(8,128)} %get-tuple-element.41.acc_ref, ...), custom_call_target="tpu_custom_call" | custom-call | flops 5637144576 | bytes 7340032 | tf_op jit(solution)/shard_map/rest/pallas_call | solution.py:170
  906.4 2.2 constant_dynamic-slice_fusion
  908.7 0.0 collective-permute-done.8.refs_6_
  908.7 0.1 collective-permute-start.10
  908.7 0.0 collective-permute-done.9.refs_7_
  908.8 1.6 collective-permute-start.11
  910.3 0.0 collective-permute-done.4.refs_1_
  910.3 1.4 collective-permute-start.12
  911.7 0.6 compare_select_fusion.order
  912.3 0.0 collective-permute-done.5.refs_2_
  912.3 0.0 collective-permute-done.6.refs_3_
  912.3 3.9 collective-permute-done.10.refs_9_
  916.2 1.3 collective-permute-done.11.refs_10_
  917.6 3.3 collective-permute-done.12.refs_11_
  920.9 0.0 copy-done.6
  920.9 9.2 join.1
  (19 shorter events, 0.1 us)
Async XLA Ops:
  0.0 9.8 %copy-start.10 = (s32[14,2]{0,1:T(2,128)S(1)}, s32[14,2]{0,1:T(2,128)}, u32[]{:S(2)}) copy-start(s32[14,2]{0,1:T(2,128)} %param.10) | copy-start | bytes 340
  3.9 103.4 %collective-permute-start = (bf16[768,1024]{1,0:T(8,128)(2,1)}, bf16[768,1024]{1,0:T(8,128)(2,1)S(1)}, u32[]{:S(2)}, u32[]{:S(2)}) collective-permute-start(bf16[768,1024]{1,0:T(8,128)(2,1)} %get-tuple-element.52), channel_id=1, source_target_pairs={{0,4},{4,8},{8,12},{12,16},{16,20},{20,24},{24,28},{1,5},{5,9},{9,... | collective-permute-start | bytes 4718600 | tf_op jit(solution)/shard_map/ppermute | solution.py:242
  7.3 100.0 %collective-permute-start.1 = (bf16[768,1024]{1,0:T(8,128)(2,1)}, bf16[768,1024]{1,0:T(8,128)(2,1)S(1)}, u32[]{:S(2)}, u32[]{:S(2)}) collective-permute-start(bf16[768,1024]{1,0:T(8,128)(2,1)} %get-tuple-element.51), channel_id=1, source_target_pairs={{4,0},{8,4},{12,8},{16,12},{20,16},{24,20},{28,24},{5,1},{9,5},{13... | collective-permute-start | bytes 4718600 | tf_op jit(solution)/shard_map/ppermute | solution.py:244
  9.9 97.3 %copy-start.8 = (s32[28]{0:T(128)}, s32[28]{0:T(128)S(1)}, u32[]{:S(2)}) copy-start(s32[28]{0:T(128)S(1)} %reshape.83.far_list) | copy-start | bytes 340
  10.2 97.1 %copy-start.9 = (s32[28]{0:T(128)}, s32[28]{0:T(128)S(1)}, u32[]{:S(2)}) copy-start(s32[28]{0:T(128)S(1)} %multiply_add_fusion.slot) | copy-start | bytes 340
  107.3 1.2 copy-start
  107.3 1.6 copy-start.1
  108.9 584.9 %all-to-all-start.1 = ((bf16[8,4,2,256,768]{4,3,2,1,0:T(8,128)(2,1)}), bf16[8,4,2,256,768]{4,3,2,1,0:T(8,128)(2,1)}, u32[]{:S(2)}, u32[]{:S(2)}) async-start(bf16[8,4,2,256,768]{4,3,2,1,0:T(8,128)(2,1)} %bitcast.8), calls=%async_computation.1 | async-start | bytes 50331648 | tf_op jit(solution)/shard_map/all_to_all | solution.py:253
  115.3 8.8 copy-start.11
  117.5 570.5 %collective-permute-start.2 = (bf16[768,1024]{1,0:T(8,128)(2,1)S(1)}, bf16[768,1024]{1,0:T(8,128)(2,1)S(1)}, u32[]{:S(2)}, u32[]{:S(2)}) collective-permute-start(bf16[768,1024]{1,0:T(8,128)(2,1)S(1)} %get-tuple-element.50), channel_id=1, source_target_pairs={{0,4},{4,8},{8,12},{12,16},{16,20},{20,24},{24,28},{1,5},{5,9},{9,... | collective-permute-start | bytes 4718600 | tf_op jit(solution)/shard_map/ppermute | solution.py:243
  122.2 571.7 %collective-permute-start.3 = (bf16[768,1024]{1,0:T(8,128)(2,1)S(1)}, bf16[768,1024]{1,0:T(8,128)(2,1)S(1)}, u32[]{:S(2)}, u32[]{:S(2)}) collective-permute-start(bf16[768,1024]{1,0:T(8,128)(2,1)S(1)} %get-tuple-element.49), channel_id=1, source_target_pairs={{4,0},{8,4},{12,8},{16,12},{20,16},{24,20},{28,24},{5,1},{9,5},{13... | collective-permute-start | bytes 4718600 | tf_op jit(solution)/shard_map/ppermute | solution.py:245
  688.0 5.8 copy-start.2
  693.9 1.2 copy-start.3
  695.0 93.7 %all-to-all-start.2 = ((bf16[8,4,2,256,128]{4,3,2,1,0:T(8,128)(2,1)}), bf16[8,4,2,256,128]{4,3,2,1,0:T(8,128)(2,1)}, u32[]{:S(2)}, u32[]{:S(2)}) async-start(bf16[8,4,2,256,128]{4,3,2,1,0:T(8,128)(2,1)} %bitcast.10), calls=%async_computation.2 | async-start | bytes 8388608 | tf_op jit(solution)/shard_map/all_to_all | solution.py:253
  788.7 97.1 %all-to-all-start.3 = ((bf16[8,4,2,256,128]{4,3,2,1,0:T(8,128)(2,1)}), bf16[8,4,2,256,128]{4,3,2,1,0:T(8,128)(2,1)}, u32[]{:S(2)}, u32[]{:S(2)}) async-start(bf16[8,4,2,256,128]{4,3,2,1,0:T(8,128)(2,1)} %bitcast.9), calls=%async_computation.3 | async-start | bytes 8388608 | tf_op jit(solution)/shard_map/all_to_all | solution.py:253
  801.0 109.3 %collective-permute-start.4 = (bf16[896,768]{1,0:T(8,128)(2,1)}, bf16[896,768]{1,0:T(8,128)(2,1)}, u32[]{:S(2)}, u32[]{:S(2)}) collective-permute-start(bf16[896,768]{1,0:T(8,128)(2,1)} %get-tuple-element.55), channel_id=1, source_target_pairs={{0,1},{1,2},{2,3},{3,0},{4,5},{5,6},{6,7},{7,4},{8,9},{9,10},{10,1... | collective-permute-start | bytes 4128776 | tf_op jit(solution)/shard_map/ppermute | solution.py:280
  801.0 111.3 %collective-permute-start.5 = (bf16[896,768]{1,0:T(8,128)(2,1)S(1)}, bf16[896,768]{1,0:T(8,128)(2,1)}, u32[]{:S(2)}, u32[]{:S(2)}) collective-permute-start(bf16[896,768]{1,0:T(8,128)(2,1)S(1)} %get-tuple-element.54), channel_id=1, source_target_pairs={{0,2},{1,3},{2,0},{3,1},{4,6},{5,7},{6,4},{7,5},{8,10},{9,11},{10,... | collective-permute-start | bytes 4128776 | tf_op jit(solution)/shard_map/ppermute | solution.py:280
  802.5 109.7 %collective-permute-start.6 = (bf16[896,768]{1,0:T(8,128)(2,1)S(1)}, bf16[896,768]{1,0:T(8,128)(2,1)}, u32[]{:S(2)}, u32[]{:S(2)}) collective-permute-start(bf16[896,768]{1,0:T(8,128)(2,1)S(1)} %get-tuple-element.53), channel_id=1, source_target_pairs={{0,3},{1,0},{2,1},{3,2},{4,7},{5,4},{6,5},{7,6},{8,11},{9,8},{10,9... | collective-permute-start | bytes 4128776 | tf_op jit(solution)/shard_map/ppermute | solution.py:280
  826.7 41.1 %collective-permute-start.7 = (bf16[896,128]{1,0:T(8,128)(2,1)S(1)}, bf16[896,128]{1,0:T(8,128)(2,1)S(1)}, u32[]{:S(2)}, u32[]{:S(2)}) collective-permute-start(bf16[896,128]{1,0:T(8,128)(2,1)S(1)} %get-tuple-element.63), channel_id=1, source_target_pairs={{0,1},{1,2},{2,3},{3,0},{4,5},{5,6},{6,7},{7,4},{8,9},{9,10},{10,1... | collective-permute-start | bytes 688136 | tf_op jit(solution)/shard_map/ppermute | solution.py:280
  826.8 81.9 %collective-permute-start.8 = (bf16[896,128]{1,0:T(8,128)(2,1)}, bf16[896,128]{1,0:T(8,128)(2,1)S(1)}, u32[]{:S(2)}, u32[]{:S(2)}) collective-permute-start(bf16[896,128]{1,0:T(8,128)(2,1)} %get-tuple-element.62), channel_id=1, source_target_pairs={{0,2},{1,3},{2,0},{3,1},{4,6},{5,7},{6,4},{7,5},{8,10},{9,11},{10,... | collective-permute-start | bytes 688136 | tf_op jit(solution)/shard_map/ppermute | solution.py:280
  867.8 38.6 %copy-start.4 = (bf16[896,128]{1,0:T(8,128)(2,1)}, bf16[896,128]{1,0:T(8,128)(2,1)S(1)}, u32[]{:S(2)}) copy-start(bf16[896,128]{1,0:T(8,128)(2,1)S(1)} %collective-permute-done.7.refs_5_) | copy-start | bytes 688132
  867.8 40.9 %collective-permute-start.9 = (bf16[896,128]{1,0:T(8,128)(2,1)}, bf16[896,128]{1,0:T(8,128)(2,1)S(1)}, u32[]{:S(2)}, u32[]{:S(2)}) collective-permute-start(bf16[896,128]{1,0:T(8,128)(2,1)} %get-tuple-element.61), channel_id=1, source_target_pairs={{0,3},{1,0},{2,1},{3,2},{4,7},{5,4},{6,5},{7,6},{8,11},{9,8},{10,9... | collective-permute-start | bytes 688136 | tf_op jit(solution)/shard_map/ppermute | solution.py:280
  908.7 12.2 %copy-start.5 = (bf16[896,128]{1,0:T(8,128)(2,1)}, bf16[896,128]{1,0:T(8,128)(2,1)S(1)}, u32[]{:S(2)}) copy-start(bf16[896,128]{1,0:T(8,128)(2,1)S(1)} %collective-permute-done.8.refs_6_) | copy-start | bytes 688132
  908.7 7.5 collective-permute-start.10
  908.7 12.1 %copy-start.6 = (bf16[896,128]{1,0:T(8,128)(2,1)}, bf16[896,128]{1,0:T(8,128)(2,1)S(1)}, u32[]{:S(2)}) copy-start(bf16[896,128]{1,0:T(8,128)(2,1)S(1)} %collective-permute-done.9.refs_7_) | copy-start | bytes 688132
  908.8 8.8 collective-permute-start.11
  910.3 10.6 %collective-permute-start.12 = (bf16[896,128]{1,0:T(8,128)(2,1)}, bf16[896,128]{1,0:T(8,128)(2,1)}, u32[]{:S(2)}, u32[]{:S(2)}) collective-permute-start(bf16[896,128]{1,0:T(8,128)(2,1)} %get-tuple-element.57), channel_id=1, source_target_pairs={{0,3},{1,0},{2,1},{3,2},{4,7},{5,4},{6,5},{7,6},{8,11},{9,8},{10,9... | collective-permute-start | bytes 688136 | tf_op jit(solution)/shard_map/ppermute | solution.py:280
  916.2 4.7 copy-start.7
